TPU v7x, 256 devices: a whole 4x4x8 slice. The times are simulated.
256 devices in a mesh: group: 16 (over x, z_hi), fsdp: 16 (over y, z_lo, core).
Axes of the slice: x: 4, y: 4, z: 8 (z_hi: 4, z_lo: 2; z = z_hi * 2 + z_lo), core: 2. Of those that a mesh axis runs over, the one named last changes fastest.
Arguments:
- params: float32 [16, 768, 5120], P('group', 'fsdp'), may hold values from -6 to 6
- moment_one: float32 [16, 768, 5120], P('group', 'fsdp'), may hold values from -4 to 4
- moment_two: float32 [16, 768, 5120], P('group', 'fsdp'), may hold values from 0.05 to 1
- hidden: bfloat16 [16, 8192, 768], P('group', 'fsdp'), may hold values from -6 to 6
- cotangent: bfloat16 [16, 8192, 5120], P('group', 'fsdp'), may hold values from -0.059814453 to 0.059814453
- token_ids: int32 [16, 8192], P('group', 'fsdp'), may hold values from 0 to 31999, as said below
- step: int32 [1], replicated, may hold values from 0 to 63
Outputs:
- mixed: float32 [16, 768, 5120], P('group', 'fsdp')
- moment_new: float32 [16, 768, 5120], P('group', 'fsdp')
- second_new: float32 [16, 768, 5120], P('group', 'fsdp')
Inputs may be any that keep to these rules, and one draw needn't show every extreme that they name: `token_ids`: token slots form padded sequences of 128 slots; each sequence holds ids of 1 or more up to a live length of at least 32 slots, then 0.
All inputs are finite; a program needn't handle non-finite values.
Results may differ from a plain program's by a relative error of at most 0.0003.
Values sent between devices are 32-bit elements; how exact they have to be, the bound alone decides.
A program may use at most 128 MiB of HBM per device.

v0:
```python
import jax
import jax.numpy as jnp
from jax import lax
from jax.sharding import PartitionSpec as P

beta_one = 0.9
beta_two = 0.95
learn_rate = 0.02
weight_decay = 0.1
epsilon = 1e-08


def shifted(value, axis, steps):
    count = lax.axis_size(axis)
    pairs = [(source, (source + steps) % count) for source in range(count)]
    return lax.ppermute(value, axis, pairs)


def adam_step(param, moment, second, grad, steps_done):
    moment_next = beta_one * moment + (1.0 - beta_one) * grad
    second_next = beta_two * second + (1.0 - beta_two) * grad * grad
    corr_one = 1.0 - jnp.power(beta_one, steps_done)
    corr_two = 1.0 - jnp.power(beta_two, steps_done)
    scaled = moment_next / corr_one / (jnp.sqrt(second_next / corr_two) + epsilon)
    return (param - learn_rate * (scaled + weight_decay * param), moment_next, second_next)


def from_partner(fresh, level):

    def make_branch(exponent):

        def moved(block):
            return shifted(block, "group", 2**exponent)

        return moved

    return lax.switch(level, [make_branch(exponent) for exponent in range(4)], fresh)


def per_device(params, moment_one, moment_two, hidden, cotangent, token_ids, step):
    hidden_rows = hidden[0]
    masked = jnp.where(token_ids[0][:, None] > 0, cotangent[0], jnp.zeros((), jnp.bfloat16))
    steps_done = (step[0] + 1).astype(jnp.float32)
    level = step[0] % 4
    grad = lax.psum_scatter(
        jnp.dot(hidden_rows.T, masked, preferred_element_type=jnp.float32),
        "fsdp",
        scatter_dimension=0,
        tiled=True,
    )
    fresh, moment_new, second_new = adam_step(
        params[0], moment_one[0], moment_two[0], grad, steps_done
    )
    mixed = 0.5 * (fresh + from_partner(fresh, level))
    return (mixed[None], moment_new[None], second_new[None])


def solution(mesh):
    placed = (
        P("group", "fsdp", None),
        P("group", "fsdp", None),
        P("group", "fsdp", None),
        P("group", "fsdp", None),
        P("group", "fsdp", None),
        P("group", "fsdp"),
        P(),
    )
    return jax.shard_map(
        per_device,
        mesh=mesh,
        in_specs=placed,
        out_specs=(P("group", "fsdp", None), P("group", "fsdp", None), P("group", "fsdp", None)),
        check_vma=False,
    )
```

profile of v0, /device:TPU:1, one launch (start us, length us, event | category | flops | bytes accessed | tf_op | source)
XLA Modules:
  0.0 268.1 jit_solution(2777252927496820827)
XLA Ops:
  7.2 0.0 copy-start
  7.2 0.0 reduce-scatter.4.cloned.1.call-start
  7.2 0.8 compare_reduce_fusion
  8.0 0.3 copy-done
  8.3 11.0 %convolution_bitcast_fusion = f32[768,5120]{0,1:T(8,128)} fusion(bf16[1,512,5120]{2,1,0:T(8,128)(2,1)} %param.15, pred[512]{0:T(512)(128)(4,1)S(1)} %compare_reduce_fusion, bf16[1,512,768]{2,1,0:T(8,128)(2,1)S(1)} %copy-done), kind=kOutput, calls=%fused_computation | convolution fusion | flops 4029153280 | bytes 21758464 | tf_op jit(solution)/shard_map/dot_general | solution.py:46
  19.3 15.7 %copy.32 = f32[768,5120]{1,0:T(8,128)} copy(f32[768,5120]{0,1:T(8,128)} %convolution_bitcast_fusion) | data formatting | bytes 31457280
  35.0 0.0 reduce-scatter.4.cloned.1.call-update
  35.1 0.0 copy-start.4
  35.9 0.4 copy-done.3
  36.2 2.0 copy.23
  38.4 2.0 copy.22
  40.4 2.0 copy.21
  42.3 169.4 %reduce-scatter.4.cloned.1.call-done = f32[48,5120]{1,0:T(8,128)} async-done(((f32[768,5120]{1,0:T(8,128)}), f32[48,5120]{1,0:T(8,128)}) %reduce-scatter.4.cloned.1.call-update) | async-done | bytes 983056
  211.7 3.0 %copy.33 = f32[48,5120]{0,1:T(8,128)} copy(f32[48,5120]{1,0:T(8,128)} %reduce-scatter.4.cloned.1.call-done) | data formatting | bytes 1966080
  214.7 8.4 %fusion.9 = (f32[1,48,5120]{1,2,0:T(8,128)}, f32[48,5120]{0,1:T(8,128)S(1)}, f32[1,48,5120]{1,2,0:T(8,128)}) fusion(f32[48,5120]{0,1:T(8,128)} %copy.33, f32[1,48,5120]{1,2,0:T(8,128)} %copy.23, f32[]{:T(128)S(6)} %sub.22, f32[]{:T(128)S(6)} %sub.21, f32[1,48,5120]{1,2,0:T(8,128)} %copy.22, f32[1,48,5120]{1,2,0:T(8,128)} %copy.21), kind=kLoop, calls=%fused_computation.15 | loop fusion | flops 3686400 | bytes 6881288 | tf_op jit(solution)/shard_map/broadcast_in_dim | solution.py:55
  223.0 27.1 %conditional.1 = (f32[48,5120]{0,1:T(8,128)}) conditional(s32[]{:T(128)} %clamp.3, (f32[48,5120]{0,1:T(8,128)S(1)}) %tuple.27, (f32[48,5120]{0,1:T(8,128)S(1)}) %tuple.27, (f32[48,5120]{0,1:T(8,128)S(1)}) %tuple.27, (f32[48,5120]{0,1:T(8,128)S(1)}) %tuple.27), branch_computations={%region_1.2_spmd, %region_2.3_spmd, %region_3.4_spmd, %region_4.5_... | conditional | bytes 7864368 | solution.py:37
  223.1 1.7 copy.40
  224.8 1.2 collective-permute-start.2
  226.0 21.2 %collective-permute-done.2 = f32[48,5120]{1,0:T(8,128)} collective-permute-done((f32[48,5120]{1,0:T(8,128)}, f32[48,5120]{1,0:T(8,128)}, u32[]{:S(2)}, u32[]{:S(2)}) %collective-permute-start.2) | collective-permute-done | bytes 983072 | tf_op jit(solution)/shard_map/cond/branch_2_fun/ppermute | solution.py:16
  247.2 3.0 %copy.36 = f32[48,5120]{0,1:T(8,128)} copy(f32[48,5120]{1,0:T(8,128)} %collective-permute-done.2) | data formatting | bytes 1966080 | tf_op jit(solution)/shard_map/cond | solution.py:37
  250.2 3.5 %multiply_bitcast_fusion = f32[1,48,5120]{1,2,0:T(8,128)} fusion(f32[48,5120]{0,1:T(8,128)S(1)} %get-tuple-element.24, f32[48,5120]{0,1:T(8,128)} %get-tuple-element.18), kind=kLoop, calls=%fused_computation.11 | loop fusion | flops 491520 | bytes 2949120 | tf_op jit(solution)/shard_map/broadcast_in_dim | solution.py:55
  253.6 2.9 %copy.29 = f32[1,48,5120]{2,1,0:T(8,128)} copy(f32[1,48,5120]{1,2,0:T(8,128)} %multiply_bitcast_fusion) | data formatting | bytes 1966080
  256.5 3.0 %copy.30 = f32[1,48,5120]{2,1,0:T(8,128)} copy(f32[1,48,5120]{1,2,0:T(8,128)} %get-tuple-element.25) | data formatting | bytes 1966080
  259.6 1.7 copy.31
  (8 shorter events, 0.0 us)
Async XLA Ops:
  7.2 1.2 copy-start
  7.2 204.5 %reduce-scatter.4.cloned.1.call-start = ((), (), s32[]{:S(2)}) async-start(), calls=%async_computation.1 | async-start | bytes 16711680
  35.0 1.2 copy-start.3
  35.1 3.3 %copy-start.4 = (f32[1,48,5120]{2,1,0:T(8,128)S(1)}, f32[1,48,5120]{2,1,0:T(8,128)}, u32[]{:S(2)}) copy-start(f32[1,48,5120]{2,1,0:T(8,128)} %param.12) | copy-start | bytes 2949124
  38.3 2.1 copy-start.5
  224.8 22.4 %collective-permute-start.2 = (f32[48,5120]{1,0:T(8,128)}, f32[48,5120]{1,0:T(8,128)}, u32[]{:S(2)}, u32[]{:S(2)}) collective-permute-start(f32[48,5120]{1,0:T(8,128)} %copy.40), channel_id=1, source_target_pairs={{0,64},{16,80},{32,96},{48,112},{64,128},{80,144},{96,160},{112,17... | collective-permute-start | bytes 2949128 | tf_op jit(solution)/shard_map/cond/branch_2_fun/ppermute | solution.py:16
  256.5 3.0 %copy-start.2 = (f32[1,48,5120]{1,2,0:T(8,128)S(1)}, f32[1,48,5120]{1,2,0:T(8,128)}, u32[]{:S(2)}) copy-start(f32[1,48,5120]{1,2,0:T(8,128)} %get-tuple-element.23) | copy-start | bytes 2949124
  256.5 4.8 %copy-start.1 = (bf16[1,512,768]{2,1,0:T(8,128)(2,1)S(1)}, bf16[1,512,768]{2,1,0:T(8,128)(2,1)}, u32[]{:S(2)}) copy-start(bf16[1,512,768]{2,1,0:T(8,128)(2,1)} %param.14) | copy-start | bytes 2359300
Sparse Core Ops, SparseCore 0:
  35.2 176.5 reduce-scatter.3
where the time goes:
time: 270 us; the launch traced here: 268 us
  waiting for transfers between devices  191 us (71%)
  local copies, waits for them, and re-layouts  37.7 us (14%)
  between operations  14.9 us (6%)
  other arithmetic  12.6 us (5%)
  matrix products  11 us (4%)
    unnamed x2, waiting for transfers between devices  169 us
    unnamed x20, local copies, waits for them, and re-layouts  33 us
    ppermute x1, waiting for transfers between devices, shifted(): return lax.ppermute(value, axis, pairs)  21.2 us
    broadcast_in_dim x2, other arithmetic, per_device(): return (mixed[None], moment_new[None], second_new[None])  11.9 us
    dot_general x1, matrix products, per_device(): jnp.dot(hidden_rows.T, masked, preferred_element_type=jnp.float32)  11 us
  transfers between devices with their start and end apart: 2, of which 2 were waited for; matrix products, arithmetic and copies ran while one was open for 2% of the time, Pallas kernels for 0%

commit v1 on v0

v1 whole, which is shorter than its diff:
```python
import functools

import jax
import jax.numpy as jnp
from jax import lax
from jax.experimental import pallas as pl
from jax.experimental.pallas import tpu as pltpu
from jax.sharding import PartitionSpec as P

MESH = pl.DeviceIdType.MESH

beta_one = 0.9
beta_two = 0.95
learn_rate = 0.02
weight_decay = 0.1
epsilon = 1e-08

LANES = 128
RING = 4


def kernel(
    distance,
    groups,
    steps,
    rows,
    corr_ref,
    ids_ref,
    params_hbm,
    one_hbm,
    two_hbm,
    hidden_hbm,
    cot_hbm,
    mixed_ref,
    one_out,
    two_out,
    hid,
    left_t,
    cot,
    par,
    one,
    two,
    snd,
    acc,
    r_core,
    r_far,
    r_left,
    r_right,
    z_snd,
    z_rcv,
    fresh,
    g_rcv,
    load_sem,
    cot_sem,
    core_s,
    core_r,
    y_s,
    y_r,
    z_s,
    z_r,
    g_s,
    g_r,
):
    group = lax.axis_index("group")
    place = lax.axis_index("fsdp")
    y = place // 4
    z = (place // 2) % 2
    core = place % 2
    y_next, y_prev, y_far = (y + 1) % RING, (y + 3) % RING, (y + 2) % RING
    right = (group, y_next * 4 + z * 2 + core)
    left = (group, y_prev * 4 + z * 2 + core)
    twin = (group, y * 4 + z * 2 + (1 - core))
    across = (group, y * 4 + (1 - z) * 2 + core)
    below = ((group + distance) % groups, place)
    above = ((group + groups - distance) % groups, place)

    hidden_load = pltpu.make_async_copy(hidden_hbm.at[0], hid, load_sem.at[0])
    hidden_load.start()

    def cot_load(k):
        columns = pl.ds(pl.multiple_of(k * 2 * LANES, 2 * LANES), 2 * LANES)
        return pltpu.make_async_copy(cot_hbm.at[0, :, columns], cot.at[k], cot_sem.at[k])

    def start_cot(k, carry):
        cot_load(k).start()
        return carry

    lax.fori_loop(0, steps, start_cot, 0)
    state_loads = [
        pltpu.make_async_copy(source.at[0], target, load_sem.at[1 + i])
        for i, (source, target) in enumerate(((params_hbm, par), (one_hbm, one), (two_hbm, two)))
    ]
    for load in state_loads:
        load.start()

    barrier = pltpu.get_barrier_semaphore()
    partners = [right, left, twin, across, below]
    if 2 * distance != groups:
        partners.append(above)
    for partner in partners:
        pl.semaphore_signal(barrier, inc=1, device_id=partner, device_id_type=MESH)

    hidden_load.wait()
    live = ids_ref[...] > 0
    half = 8 * rows
    for h in range(2):
        turned = jnp.transpose(hid[:, h * half : (h + 1) * half].astype(jnp.float32))
        turned = jnp.where(live, turned, 0.0).astype(jnp.bfloat16)
        for j in range(8):
            owner = h * 8 + j
            slot = 1 - core if owner % 2 == 0 else core
            left_t[slot, owner // 2] = turned[j * rows : (j + 1) * rows]

    pl.semaphore_wait(barrier, len(partners))

    def copy(source, target, send, recv, device):
        return pltpu.make_async_remote_copy(
            src_ref=source,
            dst_ref=target,
            send_sem=send,
            recv_sem=recv,
            device_id=device,
            device_id_type=MESH,
        )

    def core_copy(k):
        return copy(snd.at[k], r_core.at[k], core_s.at[k], core_r.at[k], twin)

    def y_copy(k, i):
        source, target, device = (
            (acc.at[k, 0, y_far], r_far.at[k, 0], right),
            (acc.at[k, 1, y_far], r_far.at[k, 1], left),
            (acc.at[k, 0, y_prev], r_right.at[k, 0], left),
            (acc.at[k, 1, y_next], r_left.at[k, 1], right),
            (acc.at[k, 0, y_next], r_left.at[k, 0], right),
            (acc.at[k, 1, y_prev], r_right.at[k, 1], left),
        )[i]
        return copy(source, target, y_s.at[k, i], y_r.at[k, i], device)

    def z_copy(k):
        return copy(z_snd.at[k], z_rcv.at[k], z_s.at[k], z_r.at[k], across)

    def g_copy(k):
        return copy(fresh.at[k], g_rcv.at[k], g_s.at[k], g_r.at[k], below)

    inv_one = corr_ref[0]
    inv_two = corr_ref[1]

    def multiply(k):
        cot_load(k).wait()
        for slot, target in ((0, snd), (1, acc)):
            product = jnp.dot(
                left_t[slot].reshape(8 * rows, left_t.shape[-1]),
                cot[k],
                preferred_element_type=jnp.float32,
            ).reshape(RING, 2, rows, 2 * LANES)
            target[k, 0] = product[..., :LANES]
            target[k, 1] = product[..., LANES:]
            if slot == 0:
                core_copy(k).start()

    def add_core(k):
        core_copy(k).wait_recv()
        acc[k] += r_core[k]
        for i in range(4):
            y_copy(k, i).start()

    def add_far(k):
        y_copy(k, 0).wait_recv()
        acc[k, 0, y_next] += r_far[k, 0]
        y_copy(k, 4).start()
        y_copy(k, 1).wait_recv()
        acc[k, 1, y_prev] += r_far[k, 1]
        y_copy(k, 5).start()

    def add_near(k):
        for i in range(2, 6):
            y_copy(k, i).wait_recv()
        for p in range(2):
            z_snd[k, p] = acc[k, p, y, 1 - z] + r_left[k, p, 1 - z] + r_right[k, p, 1 - z]
        z_copy(k).start()

    def update(k):
        z_copy(k).wait_recv()
        for p in range(2):
            columns = pl.ds(pl.multiple_of((2 * k + p) * LANES, LANES), LANES)
            grad = acc[k, p, y, z] + r_left[k, p, z] + r_right[k, p, z] + z_rcv[k, p]
            one_next = beta_one * one[:, columns] + (1.0 - beta_one) * grad
            two_next = beta_two * two[:, columns] + (1.0 - beta_two) * grad * grad
            one_out[0, :, columns] = one_next
            two_out[0, :, columns] = two_next
            scaled = (one_next * inv_one) / (jnp.sqrt(two_next * inv_two) + epsilon)
            held = par[:, columns]
            fresh[k, p] = held - learn_rate * (scaled + weight_decay * held)
        g_copy(k).start()

    def mix(k):
        g_copy(k).wait_recv()
        for p in range(2):
            columns = pl.ds(pl.multiple_of((2 * k + p) * LANES, LANES), LANES)
            mixed_ref[0, :, columns] = 0.5 * (fresh[k, p] + g_rcv[k, p])
        core_copy(k).wait_send()
        for i in range(6):
            y_copy(k, i).wait_send()
        z_copy(k).wait_send()
        g_copy(k).wait_send()

    stages = ((multiply, 0), (add_core, 1), (add_far, 2), (add_near, 4), (update, 5), (mix, 7))

    for load in state_loads:
        load.wait()

    def body(t, carry):
        for stage, lag in stages:

            @pl.when((t >= lag) & (t < steps + lag))
            def _(stage=stage, lag=lag):
                stage(t - lag)

        return carry

    lax.fori_loop(0, steps + stages[-1][1], body, 0)


def fused(distance, groups, corr, token_ids, params, moment_one, moment_two, hidden, cotangent):
    _, rows, width = params.shape
    _, tokens, bucket = hidden.shape
    steps = width // (2 * LANES)
    f32 = jnp.float32
    whole = pltpu.VMEM((steps, 2, RING, 2, rows, LANES), f32)
    unit = pltpu.VMEM((steps, 2, 2, rows, LANES), f32)
    own = pltpu.VMEM((steps, 2, rows, LANES), f32)
    shard = pltpu.VMEM((rows, width), f32)
    dma = pltpu.SemaphoreType.DMA
    out = jax.ShapeDtypeStruct(params.shape, f32)
    anywhere = pl.BlockSpec(memory_space=pl.ANY)
    vmem = pl.BlockSpec(memory_space=pltpu.VMEM)
    return pl.pallas_call(
        functools.partial(kernel, distance, groups, steps, rows),
        out_shape=(out, out, out),
        in_specs=[pl.BlockSpec(memory_space=pltpu.SMEM), vmem] + [anywhere] * 5,
        out_specs=(vmem, vmem, vmem),
        scratch_shapes=[
            pltpu.VMEM((tokens, bucket), jnp.bfloat16),
            pltpu.VMEM((2, 8, rows, tokens), jnp.bfloat16),
            pltpu.VMEM((steps, tokens, 2 * LANES), jnp.bfloat16),
            shard,
            shard,
            shard,
            whole,
            whole,
            whole,
            unit,
            unit,
            unit,
            own,
            own,
            own,
            own,
            dma((4,)),
            dma((steps,)),
            dma((steps,)),
            dma((steps,)),
            dma((steps, 6)),
            dma((steps, 6)),
            dma((steps,)),
            dma((steps,)),
            dma((steps,)),
            dma((steps,)),
        ],
        compiler_params=pltpu.CompilerParams(
            collective_id=distance.bit_length(),
            has_side_effects=True,
            vmem_limit_bytes=60 * 1024 * 1024,
        ),
        cost_estimate=pl.CostEstimate(
            flops=2 * tokens * bucket * width,
            bytes_accessed=2 * tokens * (bucket + width) + 24 * rows * width,
            transcendentals=rows * width,
        ),
    )(corr, token_ids, params, moment_one, moment_two, hidden, cotangent)


def solution(mesh):
    groups = mesh.shape["group"]

    def per_device(params, moment_one, moment_two, hidden, cotangent, token_ids, step):
        steps_done = (step[0] + 1).astype(jnp.float32)
        corr = jnp.stack(
            [
                1.0 / (1.0 - jnp.power(beta_one, steps_done)),
                1.0 / (1.0 - jnp.power(beta_two, steps_done)),
            ]
        )
        branches = [functools.partial(fused, 2**level, groups) for level in range(4)]
        return lax.switch(
            step[0] % 4,
            branches,
            corr,
            token_ids,
            params,
            moment_one,
            moment_two,
            hidden,
            cotangent,
        )

    rows = P("group", "fsdp", None)
    return jax.shard_map(
        per_device,
        mesh=mesh,
        in_specs=(rows, rows, rows, rows, rows, P("group", "fsdp"), P()),
        out_specs=(rows, rows, rows),
        check_vma=False,
    )
```

time: 270 us -> 91.1 us (0.34)
  waiting for transfers between devices: 191 us -> 0 us
  Pallas kernels: 0 us -> 86.7 us
  local copies, waits for them, and re-layouts: 37.7 us -> 2.83 us
  between operations: 14.9 us -> 1.47 us
  other arithmetic: 12.6 us -> 0.08 us
  matrix products: 11 us -> 0 us
    unnamed x2 -> x0, waiting for transfers between devices: 169 us -> none
    pallas_call x0 -> x1, Pallas kernels: none -> 86.7 us  [fused(): pl.pallas_call(functools.partial(kernel, distance, groups, steps, rows),...]
    unnamed x20 -> x3, local copies, waits for them, and re-layouts: 33 us -> 2.83 us
    ppermute x1 -> x0, waiting for transfers between devices: 21.2 us -> none  [shifted(): return lax.ppermute(value, axis, pairs)]
    broadcast_in_dim x2 -> x0, other arithmetic: 11.9 us -> none  [per_device(): return (mixed[None], moment_new[None], second_new[None])]
    dot_general x1 -> x0, matrix products: 11 us -> none  [per_device(): jnp.dot(hidden_rows.T, masked, preferred_element_type=jnp.float32)]
    cond x1 -> x0, local copies, waits for them, and re-layouts: 2.96 us -> none  [from_partner(): lax.switch(level, [make_branch(exponent) for exponent in range(4)], fresh)]
  transfers between devices with their start and end apart: 2 -> 0, of which waited for: 2 -> 0; matrix products, arithmetic and copies ran while one was open for 2% -> 0% of each run, Pallas kernels for 0% -> 0%
where the time goes in v1:
time: 91.1 us; the launch traced here: 91 us
  Pallas kernels  86.7 us (95%)
  local copies, waits for them, and re-layouts  2.83 us (3%)
  between operations  1.47 us (2%)
    pallas_call x1, Pallas kernels, fused(): pl.pallas_call(functools.partial(kernel, distance, groups, steps, rows),...  86.7 us
    unnamed x3, local copies, waits for them, and re-layouts  2.83 us

profile of v1, /device:TPU:1, one launch (start us, length us, event | category | flops | bytes accessed | tf_op | source)
XLA Modules:
  0.0 91.0 jit_solution(5158378175721349635)
XLA Ops:
  1.5 0.1 pad_maximum_fusion
  1.5 86.7 %conditional.1 = ((f32[1,48,5120]{2,1,0:T(8,128)S(1)}, f32[1,48,5120]{2,1,0:T(8,128)S(1)}, f32[1,48,5120]{2,1,0:T(8,128)S(1)})) conditional(s32[]{:T(128)} %clamp.3, (f32[2]{0:T(128)S(1)}, s32[1,512]{1,0:T(1,128)}, f32[1,48,5120]{2,1,0:T(8,128)}, f32[1,48,5120]{2,1,0:T(8,128)}, f32[1,48,5120]{2,1,0:T(8,128)}, ...), branch_computations={%region_0.1_spmd, %region_1.2_spmd, %region_2.3_spmd, %region_3.4_... | conditional | flops 4026531840 | bytes 11927560 | solution.py:296
  1.5 86.7 %branch_3_fun.1 = (f32[1,48,5120]{2,1,0:T(8,128)S(1)}, f32[1,48,5120]{2,1,0:T(8,128)S(1)}, f32[1,48,5120]{2,1,0:T(8,128)S(1)}) custom-call(f32[2]{0:T(128)S(1)} %get-tuple-element.77.corr_ref, s32[1,512]{1,0:T(1,128)} %get-tuple-element.129.ids_ref, f32[1,48,5120]{2,1,0:T(8,128)} %get-tuple-element.133.params_hbm, ...), custom_call_target="tpu_custom_call" | custom-call | flops 4026531840 | bytes 11927552 | tf_op jit(solution)/shard_map/cond/branch_3_fun/pallas_call | solution.py:238
  88.2 0.9 %copy.62 = f32[1,48,5120]{2,1,0:T(8,128)} copy(f32[1,48,5120]{2,1,0:T(8,128)S(1)} %get-tuple-element.165) | data formatting | bytes 1966080
  89.1 0.9 %copy.63 = f32[1,48,5120]{2,1,0:T(8,128)} copy(f32[1,48,5120]{2,1,0:T(8,128)S(1)} %get-tuple-element.166) | data formatting | bytes 1966080
  90.1 0.9 %copy.64 = f32[1,48,5120]{2,1,0:T(8,128)} copy(f32[1,48,5120]{2,1,0:T(8,128)S(1)} %get-tuple-element.167) | data formatting | bytes 1966080

commit v2 on v1

v2 whole, which is shorter than its diff:
```python
import functools

import jax
import jax.numpy as jnp
from jax import lax
from jax.experimental import pallas as pl
from jax.experimental.pallas import tpu as pltpu
from jax.sharding import PartitionSpec as P

MESH = pl.DeviceIdType.MESH

beta_one = 0.9
beta_two = 0.95
learn_rate = 0.02
weight_decay = 0.1
epsilon = 1e-08

LANES = 128
RING = 4
PREFETCH = 8
EARLY = {1: 6, 2: 6, 4: 3, 8: 3}
STEP_BITS = 16

PLANS = {
    1: (0, (0, 3, 6, 9, 11, 15), ()),
    2: (0, (0, 4, 8, 12, 15, 20), ()),
    4: (18, (0, 2, 5, 8, 11, 15), (0, 2, 6, 9, 12, 16)),
    8: (18, (0, 2, 5, 8, 11, 15), (0, 2, 6, 9, 12, 16)),
}


def power(base, exponent):
    result = jnp.float32(1.0)
    for bit in range(STEP_BITS):
        factor = jnp.float32(base ** (2**bit))
        result = result * jnp.where((exponent >> bit) & 1 == 1, factor, jnp.float32(1.0))
    return result


def kernel(
    distance,
    groups,
    chunks,
    rows,
    step_ref,
    ids_ref,
    params_hbm,
    one_hbm,
    two_hbm,
    hidden_hbm,
    cot_hbm,
    mixed_ref,
    one_out,
    two_out,
    hid,
    left_t,
    cot,
    par,
    one,
    two,
    snd,
    acc,
    r_core,
    y_far_in,
    y_b_in,
    y_c_in,
    z_snd,
    z_rcv,
    q_z_in,
    q_far_in,
    q_b_in,
    q_c_in,
    fresh,
    g_rcv,
    load_sem,
    cot_sem,
    core_s,
    core_r,
    y_s,
    y_r,
    z_s,
    z_r,
    g_s,
    g_r,
):
    z_first, y_lags, q_lags = PLANS[distance]
    y_first = chunks - z_first

    group = lax.axis_index("group")
    place = lax.axis_index("fsdp")
    y = place // 4
    z = (place // 2) % 2
    core = place % 2
    far = (y + 2) % RING

    def along(other_y):
        return (group, other_y * 4 + z * 2 + core)

    twin = (group, y * 4 + z * 2 + (1 - core))
    across = (group, y * 4 + (1 - z) * 2 + core)
    below = ((group + distance) % groups, place)
    above = ((group + groups - distance) % groups, place)

    barrier = pltpu.get_barrier_semaphore()
    partners = [along((y + 1) % RING), along((y + 3) % RING), twin, across, below]
    if 2 * distance != groups:
        partners.append(above)
    for partner in partners:
        pl.semaphore_signal(barrier, inc=1, device_id=partner, device_id_type=MESH)

    hidden_load = pltpu.make_async_copy(hidden_hbm.at[0], hid, load_sem.at[0])
    hidden_load.start()

    def cot_load(k):
        columns = pl.ds(pl.multiple_of(k * LANES, LANES), LANES)
        return pltpu.make_async_copy(cot_hbm.at[0, :, columns], cot.at[k], cot_sem.at[k])

    streams = [(0, y_first)] + ([(y_first, z_first)] if z_first else [])
    for base, count in streams:
        for k in range(min(PREFETCH, count)):
            cot_load(base + k).start()
    state_loads = [
        pltpu.make_async_copy(source.at[0], target, load_sem.at[1 + i])
        for i, (source, target) in enumerate(((params_hbm, par), (one_hbm, one), (two_hbm, two)))
    ]

    done = step_ref[0] + 1
    inv_one = 1.0 / (1.0 - jnp.full((1, LANES), power(beta_one, done)))
    inv_two = 1.0 / (1.0 - jnp.full((1, LANES), power(beta_two, done)))

    hidden_load.wait()
    live = ids_ref[...] > 0
    half = 8 * rows
    for h in range(2):
        turned = jnp.transpose(hid[:, h * half : (h + 1) * half].astype(jnp.float32))
        turned = jnp.where(live, turned, 0.0).astype(jnp.bfloat16)
        for j in range(8):
            owner = h * 8 + j
            slot = 1 - core if owner % 2 == 0 else core
            left_t[slot, owner // 2] = turned[j * rows : (j + 1) * rows]

    for load in state_loads:
        load.start()

    def copy(source, target, send, recv, device):
        return pltpu.make_async_remote_copy(
            src_ref=source,
            dst_ref=target,
            send_sem=send,
            recv_sem=recv,
            device_id=device,
            device_id_type=MESH,
        )

    def columns_of(k):
        return pl.ds(pl.multiple_of(k * LANES, LANES), LANES)

    def core_copy(k):
        return copy(snd.at[k], r_core.at[k], core_s.at[k], core_r.at[k], twin)

    def g_copy(k):
        return copy(fresh.at[k], g_rcv.at[k], g_s.at[k], g_r.at[k], below)

    def multiply(k, z_major, send=True):
        cot_load(k).wait()
        for slot, target in ((0, snd), (1, acc)):
            product = jnp.dot(
                left_t[slot].reshape(8 * rows, left_t.shape[-1]),
                cot[k],
                preferred_element_type=jnp.float32,
            )
            for block in range(8):
                there = (block % 2) * RING + block // 2 if z_major else block
                target[k, there] = product[block * rows : (block + 1) * rows]
            if slot == 0 and send:
                core_copy(k).start()

    def prefetch(k, end):
        @pl.when(k + PREFETCH < end)
        def _():
            cot_load(k + PREFETCH).start()

    def adam(k, grad):
        columns = columns_of(k)
        one_next = beta_one * one[:, columns] + (1.0 - beta_one) * grad
        two_next = beta_two * two[:, columns] + (1.0 - beta_two) * grad * grad
        one_out[0, :, columns] = one_next
        two_out[0, :, columns] = two_next
        scaled = (one_next * inv_one) / (jnp.sqrt(two_next * inv_two) + epsilon)
        held = par[:, columns]
        fresh[k] = held - learn_rate * (scaled + weight_decay * held)
        g_copy(k).start()

    def ring_of(parity):
        return (y + 1 + 2 * parity) % RING, (y + 3 + 2 * parity) % RING

    def mixing(k):
        g_copy(k).wait_recv()
        mixed_ref[0, :, columns_of(k)] = 0.5 * (fresh[k] + g_rcv[k])
        core_copy(k).wait_send()
        g_copy(k).wait_send()

    def y_copies(k):
        to_c, to_b = ring_of(k % 2)

        def of(other):
            return acc.at[k, pl.ds(other * 2, 2)]

        return (
            copy(of(far), y_far_in.at[k], y_s.at[k, 0], y_r.at[k, 0], along(to_c)),
            copy(of(to_b), y_b_in.at[k], y_s.at[k, 1], y_r.at[k, 1], along(to_b)),
            copy(of(to_c), y_c_in.at[k], y_s.at[k, 2], y_r.at[k, 2], along(to_c)),
        )

    def z_copy(k):
        return copy(z_snd.at[k], z_rcv.at[k], z_s.at[k], z_r.at[k], across)

    def y_multiply(k, send=True):
        prefetch(k, y_first)
        multiply(k, False, send)

    def y_core(k):
        core_copy(k).wait_recv()
        acc[k] += r_core[k]
        by_far, by_b, _ = y_copies(k)
        by_far.start()
        by_b.start()

    def y_merge(k):
        by_far, _, by_c = y_copies(k)
        to_c, _ = ring_of(k % 2)
        by_far.wait_recv()
        acc[k, pl.ds(to_c * 2, 2)] += y_far_in[k]
        by_c.start()

    def y_near(k):
        _, by_b, by_c = y_copies(k)
        by_b.wait_recv()
        by_c.wait_recv()
        z_snd[k] = acc[k, y * 2 + 1 - z] + y_b_in[k, 1 - z] + y_c_in[k, 1 - z]
        z_copy(k).start()

    def y_update(k):
        z_copy(k).wait_recv()
        adam(k, acc[k, y * 2 + z] + y_b_in[k, z] + y_c_in[k, z] + z_rcv[k])

    def y_mix(k):
        mixing(k)
        for moved in y_copies(k):
            moved.wait_send()
        z_copy(k).wait_send()

    def q_z_copy(k):
        j = k - y_first
        return copy(
            acc.at[k, pl.ds((1 - z) * RING, RING)], q_z_in.at[j], z_s.at[k], z_r.at[k], across
        )

    def q_copies(k):
        j = k - y_first
        to_c, to_b = ring_of((j + 1) % 2)

        def of(other):
            return acc.at[k, z * RING + other]

        return (
            copy(of(far), q_far_in.at[j], y_s.at[k, 0], y_r.at[k, 0], along(to_c)),
            copy(of(to_b), q_b_in.at[j], y_s.at[k, 1], y_r.at[k, 1], along(to_b)),
            copy(of(to_c), q_c_in.at[j], y_s.at[k, 2], y_r.at[k, 2], along(to_c)),
        )

    def q_multiply(k, send=True):
        prefetch(k, chunks)
        multiply(k, True, send)

    def q_core(k):
        core_copy(k).wait_recv()
        acc[k] += r_core[k]
        q_z_copy(k).start()

    def q_across(k):
        q_z_copy(k).wait_recv()
        acc[k, pl.ds(z * RING, RING)] += q_z_in[k - y_first]
        by_far, by_b, _ = q_copies(k)
        by_far.start()
        by_b.start()

    def q_merge(k):
        by_far, _, by_c = q_copies(k)
        to_c, _ = ring_of((k - y_first + 1) % 2)
        by_far.wait_recv()
        acc[k, z * RING + to_c] += q_far_in[k - y_first]
        by_c.start()

    def q_update(k):
        _, by_b, by_c = q_copies(k)
        by_b.wait_recv()
        by_c.wait_recv()
        j = k - y_first
        adam(k, acc[k, z * RING + y] + q_b_in[j] + q_c_in[j])

    def q_mix(k):
        mixing(k)
        for moved in q_copies(k):
            moved.wait_send()
        q_z_copy(k).wait_send()

    work = [(0, y_first, *pair) for pair in zip((y_multiply, y_core, y_merge, y_near, y_update, y_mix), y_lags)]
    if z_first:
        more = [(y_first, z_first, *pair) for pair in zip((q_multiply, q_core, q_across, q_merge, q_update, q_mix), q_lags)]
        work = [entry for both in zip(work, more) for entry in both]

    early = EARLY[distance]

    def ahead(k, carry):
        y_multiply(k, False)
        if z_first:
            q_multiply(y_first + k, False)
        return carry

    lax.fori_loop(0, early, ahead, 0)
    pl.semaphore_wait(barrier, len(partners))

    def first_core(k, carry):
        for base, _ in streams:
            core_copy(base + k).start()
        return carry

    lax.fori_loop(0, early, first_core, 0)

    def body(t, carry):
        @pl.when(t == early)
        def _():
            for load in state_loads:
                load.wait()

        for base, count, stage, lag in work:

            @pl.when((t >= max(lag, early if lag == 0 else 0)) & (t < count + lag))
            def _(base=base, stage=stage, lag=lag):
                stage(base + t - lag)

        return carry

    first = min(lag for _, _, _, lag in work if lag)
    lax.fori_loop(first, max(count + lag for _, count, _, lag in work), body, 0)


def written(one_ref, two_ref, three_ref, one_out, two_out, three_out, sems):
    moves = [
        pltpu.make_async_copy(source, target, sems.at[i])
        for i, (source, target) in enumerate(((one_ref, one_out), (two_ref, two_out), (three_ref, three_out)))
    ]
    for move in moves:
        move.start()
    for move in moves:
        move.wait()


def write_out(*arrays):
    return pl.pallas_call(
        written,
        out_shape=tuple(jax.ShapeDtypeStruct(array.shape, array.dtype) for array in arrays),
        in_specs=[pl.BlockSpec(memory_space=pl.ANY)] * 3,
        out_specs=(pl.BlockSpec(memory_space=pl.ANY),) * 3,
        scratch_shapes=[pltpu.SemaphoreType.DMA((3,))],
        compiler_params=pltpu.CompilerParams(vmem_limit_bytes=1024 * 1024),
    )(*arrays)


def fused(distance, groups, step, token_ids, params, moment_one, moment_two, hidden, cotangent):
    _, rows, width = params.shape
    _, tokens, bucket = hidden.shape
    chunks = width // LANES
    z_first = PLANS[distance][0]
    y_first, z_slots = chunks - z_first, max(z_first, 1)
    f32 = jnp.float32
    dma = pltpu.SemaphoreType.DMA
    whole = pltpu.VMEM((chunks, 8, rows, LANES), f32)
    shard = pltpu.VMEM((rows, width), f32)
    own = pltpu.VMEM((chunks, rows, LANES), f32)
    unit = pltpu.VMEM((y_first, 2, rows, LANES), f32)
    single = pltpu.VMEM((y_first, rows, LANES), f32)
    q_single = pltpu.VMEM((z_slots, rows, LANES), f32)
    out = jax.ShapeDtypeStruct(params.shape, f32)
    anywhere = pl.BlockSpec(memory_space=pl.ANY)
    vmem = pl.BlockSpec(memory_space=pltpu.VMEM)
    return pl.pallas_call(
        functools.partial(kernel, distance, groups, chunks, rows),
        out_shape=(out, out, out),
        in_specs=[pl.BlockSpec(memory_space=pltpu.SMEM), vmem] + [anywhere] * 5,
        out_specs=(vmem, vmem, vmem),
        scratch_shapes=[
            pltpu.VMEM((tokens, bucket), jnp.bfloat16),
            pltpu.VMEM((2, 8, rows, tokens), jnp.bfloat16),
            pltpu.VMEM((chunks, tokens, LANES), jnp.bfloat16),
            shard,
            shard,
            shard,
            whole,
            whole,
            whole,
            unit,
            unit,
            unit,
            single,
            single,
            pltpu.VMEM((z_slots, RING, rows, LANES), f32),
            q_single,
            q_single,
            q_single,
            own,
            own,
            dma((4,)),
            dma((chunks,)),
            dma((chunks,)),
            dma((chunks,)),
            dma((chunks, 3)),
            dma((chunks, 3)),
            dma((chunks,)),
            dma((chunks,)),
            dma((chunks,)),
            dma((chunks,)),
        ],
        compiler_params=pltpu.CompilerParams(
            collective_id=distance.bit_length(),
            has_side_effects=True,
            vmem_limit_bytes=58 * 1024 * 1024,
        ),
        cost_estimate=pl.CostEstimate(
            flops=2 * tokens * bucket * width,
            bytes_accessed=2 * tokens * (bucket + width) + 24 * rows * width,
            transcendentals=rows * width,
        ),
    )(step, token_ids, params, moment_one, moment_two, hidden, cotangent)


def solution(mesh):
    groups = mesh.shape["group"]

    def per_device(params, moment_one, moment_two, hidden, cotangent, token_ids, step):
        branches = [functools.partial(fused, 2**level, groups) for level in range(4)]
        operands = (step, token_ids, params, moment_one, moment_two, hidden, cotangent)
        return write_out(*lax.switch(step[0] & 3, branches, *operands))

    rows = P("group", "fsdp", None)
    return jax.shard_map(
        per_device,
        mesh=mesh,
        in_specs=(rows, rows, rows, rows, rows, P("group", "fsdp"), P()),
        out_specs=(rows, rows, rows),
        check_vma=False,
    )
```

time: 91.1 us -> 102 us (1.12)
  Pallas kernels: 86.7 us -> 101 us
  local copies, waits for them, and re-layouts: 2.83 us -> 0 us
    pallas_call x1 -> x2, Pallas kernels: 86.7 us -> 101 us  [the longest x1 99 us: fused(): pl.pallas_call(functools.partial(kernel, distance, groups, chunks, rows),...]
    unnamed x3 -> x0, local copies, waits for them, and re-layouts: 2.83 us -> none
where the time goes in v2:
time: 102 us
  Pallas kernels  101 us (99%)
  between operations  1.29 us (1%)
    pallas_call x1, Pallas kernels, fused(): pl.pallas_call(functools.partial(kernel, distance, groups, chunks, rows),...  99 us

profile of v2, /device:TPU:1, one launch (start us, length us, event | category | flops | bytes accessed | tf_op | source)
XLA Modules:
  0.0 101.9 jit_solution(187507555614432760)
XLA Ops:
  1.3 99.0 %conditional.1 = ((f32[1,48,5120]{2,1,0:T(8,128)S(1)}, f32[1,48,5120]{2,1,0:T(8,128)S(1)}, f32[1,48,5120]{2,1,0:T(8,128)S(1)})) conditional(s32[]{:T(128)} %bitcast, (s32[1]{0:T(128)}, s32[1,512]{1,0:T(1,128)}, f32[1,48,5120]{2,1,0:T(8,128)}, f32[1,48,5120]{2,1,0:T(8,128)}, f32[1,48,5120]{2,1,0:T(8,128)}, ...), branch_computations={%region_0.0_spmd, %region_1.0_spmd, %region_2.0_spmd, %region_3.0_... | conditional | flops 4026531840 | bytes 11927560 | solution.py:444
  1.3 99.0 %branch_1_fun.1 = (f32[1,48,5120]{2,1,0:T(8,128)S(1)}, f32[1,48,5120]{2,1,0:T(8,128)S(1)}, f32[1,48,5120]{2,1,0:T(8,128)S(1)}) custom-call(s32[1]{0:T(128)} %get-tuple-element.63.step_ref, s32[1,512]{1,0:T(1,128)} %get-tuple-element.64.ids_ref, f32[1,48,5120]{2,1,0:T(8,128)} %get-tuple-element.65.params_hbm, f32[1,48,5120]{2,1,0:T(8,128)} %get-tuple-element.66.one_hbm, ...), custom_call_target="tpu_custom_call" | custom-call | flops 4026531840 | bytes 11927552 | tf_op jit(solution)/shard_map/cond/branch_1_fun/pallas_call | solution.py:388
  100.3 1.6 %shard_map.94 = (f32[1,48,5120]{2,1,0:T(8,128)}, f32[1,48,5120]{2,1,0:T(8,128)}, f32[1,48,5120]{2,1,0:T(8,128)}) custom-call(f32[1,48,5120]{2,1,0:T(8,128)S(1)} %get-tuple-element.90.one_ref, f32[1,48,5120]{2,1,0:T(8,128)S(1)} %get-tuple-element.91.two_ref, f32[1,48,5120]{2,1,0:T(8,128)S(1)} %get-tuple-element.92.three_ref), custom_call_target="tpu_custom_call" | custom-call | tf_op jit(solution)/shard_map/pallas_call | solution.py:361

commit v3 on v2

--- a/solution.py
+++ b/solution.py
@@ -20,6 +20,7 @@
 PREFETCH = 8
 EARLY = {1: 6, 2: 6, 4: 3, 8: 3}
 STEP_BITS = 16
+SPAN = 5
 
 PLANS = {
     1: (0, (0, 3, 6, 9, 11, 15), ()),
@@ -62,25 +63,21 @@
     acc,
     r_core,
     y_far_in,
-    y_b_in,
-    y_c_in,
+    y_near_in,
     z_snd,
     z_rcv,
     q_z_in,
     q_far_in,
-    q_b_in,
-    q_c_in,
+    q_near_in,
     fresh,
     g_rcv,
     load_sem,
     cot_sem,
-    core_s,
+    sent,
     core_r,
-    y_s,
-    y_r,
-    z_s,
+    far_r,
+    near_r,
     z_r,
-    g_s,
     g_r,
 ):
     z_first, y_lags, q_lags = PLANS[distance]
@@ -112,8 +109,9 @@
     hidden_load.start()
 
     def cot_load(k):
+        slot = jnp.where(k < y_first, k % PREFETCH, PREFETCH + (k - y_first) % PREFETCH)
         columns = pl.ds(pl.multiple_of(k * LANES, LANES), LANES)
-        return pltpu.make_async_copy(cot_hbm.at[0, :, columns], cot.at[k], cot_sem.at[k])
+        return pltpu.make_async_copy(cot_hbm.at[0, :, columns], cot.at[k], cot_sem.at[slot])
 
     streams = [(0, y_first)] + ([(y_first, z_first)] if z_first else [])
     for base, count in streams:
@@ -142,11 +140,11 @@
     for load in state_loads:
         load.start()
 
-    def copy(source, target, send, recv, device):
+    def copy(k, source, target, recv, device):
         return pltpu.make_async_remote_copy(
             src_ref=source,
             dst_ref=target,
-            send_sem=send,
+            send_sem=sent.at[k // SPAN],
             recv_sem=recv,
             device_id=device,
             device_id_type=MESH,
@@ -156,13 +154,19 @@
         return pl.ds(pl.multiple_of(k * LANES, LANES), LANES)
 
     def core_copy(k):
-        return copy(snd.at[k], r_core.at[k], core_s.at[k], core_r.at[k], twin)
+        return copy(k, snd.at[k], r_core.at[k], core_r.at[k], twin)
 
     def g_copy(k):
-        return copy(fresh.at[k], g_rcv.at[k], g_s.at[k], g_r.at[k], below)
-
-    def multiply(k, z_major, send=True):
+        return copy(k, fresh.at[k], g_rcv.at[k], g_r.at[k], below)
+
+    def prefetch(k, end):
+        @pl.when(k + PREFETCH < end)
+        def _():
+            cot_load(k + PREFETCH).start()
+
+    def multiply(k, end, z_major, send):
         cot_load(k).wait()
+        prefetch(k, end)
         for slot, target in ((0, snd), (1, acc)):
             product = jnp.dot(
                 left_t[slot].reshape(8 * rows, left_t.shape[-1]),
@@ -175,11 +179,6 @@
             if slot == 0 and send:
                 core_copy(k).start()
 
-    def prefetch(k, end):
-        @pl.when(k + PREFETCH < end)
-        def _():
-            cot_load(k + PREFETCH).start()
-
     def adam(k, grad):
         columns = columns_of(k)
         one_next = beta_one * one[:, columns] + (1.0 - beta_one) * grad
@@ -197,8 +196,6 @@
     def mixing(k):
         g_copy(k).wait_recv()
         mixed_ref[0, :, columns_of(k)] = 0.5 * (fresh[k] + g_rcv[k])
-        core_copy(k).wait_send()
-        g_copy(k).wait_send()
 
     def y_copies(k):
         to_c, to_b = ring_of(k % 2)
@@ -207,17 +204,19 @@
             return acc.at[k, pl.ds(other * 2, 2)]
 
         return (
-            copy(of(far), y_far_in.at[k], y_s.at[k, 0], y_r.at[k, 0], along(to_c)),
-            copy(of(to_b), y_b_in.at[k], y_s.at[k, 1], y_r.at[k, 1], along(to_b)),
-            copy(of(to_c), y_c_in.at[k], y_s.at[k, 2], y_r.at[k, 2], along(to_c)),
+            copy(k, of(far), y_far_in.at[k], far_r.at[k], along(to_c)),
+            copy(k, of(to_b), y_near_in.at[k, 0], near_r.at[k], along(to_b)),
+            copy(k, of(to_c), y_near_in.at[k, 1], near_r.at[k], along(to_c)),
         )
 
+    def near_arrived(k, both):
+        copy(k, both, both, near_r.at[k], twin).wait_recv()
+
     def z_copy(k):
-        return copy(z_snd.at[k], z_rcv.at[k], z_s.at[k], z_r.at[k], across)
+        return copy(k, z_snd.at[k], z_rcv.at[k], z_r.at[k], across)
 
     def y_multiply(k, send=True):
-        prefetch(k, y_first)
-        multiply(k, False, send)
+        multiply(k, y_first, False, send)
 
     def y_core(k):
         core_copy(k).wait_recv()
@@ -234,27 +233,17 @@
         by_c.start()
 
     def y_near(k):
-        _, by_b, by_c = y_copies(k)
-        by_b.wait_recv()
-        by_c.wait_recv()
-        z_snd[k] = acc[k, y * 2 + 1 - z] + y_b_in[k, 1 - z] + y_c_in[k, 1 - z]
+        near_arrived(k, y_near_in.at[k])
+        z_snd[k] = acc[k, y * 2 + 1 - z] + y_near_in[k, 0, 1 - z] + y_near_in[k, 1, 1 - z]
         z_copy(k).start()
 
     def y_update(k):
         z_copy(k).wait_recv()
-        adam(k, acc[k, y * 2 + z] + y_b_in[k, z] + y_c_in[k, z] + z_rcv[k])
-
-    def y_mix(k):
-        mixing(k)
-        for moved in y_copies(k):
-            moved.wait_send()
-        z_copy(k).wait_send()
+        adam(k, acc[k, y * 2 + z] + y_near_in[k, 0, z] + y_near_in[k, 1, z] + z_rcv[k])
 
     def q_z_copy(k):
         j = k - y_first
-        return copy(
-            acc.at[k, pl.ds((1 - z) * RING, RING)], q_z_in.at[j], z_s.at[k], z_r.at[k], across
-        )
+        return copy(k, acc.at[k, pl.ds((1 - z) * RING, RING)], q_z_in.at[j], z_r.at[k], across)
 
     def q_copies(k):
         j = k - y_first
@@ -264,14 +253,13 @@
             return acc.at[k, z * RING + other]
 
         return (
-            copy(of(far), q_far_in.at[j], y_s.at[k, 0], y_r.at[k, 0], along(to_c)),
-            copy(of(to_b), q_b_in.at[j], y_s.at[k, 1], y_r.at[k, 1], along(to_b)),
-            copy(of(to_c), q_c_in.at[j], y_s.at[k, 2], y_r.at[k, 2], along(to_c)),
+            copy(k, of(far), q_far_in.at[j], far_r.at[k], along(to_c)),
+            copy(k, of(to_b), q_near_in.at[j, 0], near_r.at[k], along(to_b)),
+            copy(k, of(to_c), q_near_in.at[j, 1], near_r.at[k], along(to_c)),
         )
 
     def q_multiply(k, send=True):
-        prefetch(k, chunks)
-        multiply(k, True, send)
+        multiply(k, chunks, True, send)
 
     def q_core(k):
         core_copy(k).wait_recv()
@@ -293,21 +281,13 @@
         by_c.start()
 
     def q_update(k):
-        _, by_b, by_c = q_copies(k)
-        by_b.wait_recv()
-        by_c.wait_recv()
         j = k - y_first
-        adam(k, acc[k, z * RING + y] + q_b_in[j] + q_c_in[j])
-
-    def q_mix(k):
-        mixing(k)
-        for moved in q_copies(k):
-            moved.wait_send()
-        q_z_copy(k).wait_send()
-
-    work = [(0, y_first, *pair) for pair in zip((y_multiply, y_core, y_merge, y_near, y_update, y_mix), y_lags)]
+        near_arrived(k, q_near_in.at[j])
+        adam(k, acc[k, z * RING + y] + q_near_in[j, 0] + q_near_in[j, 1])
+
+    work = [(0, y_first, *pair) for pair in zip((y_multiply, y_core, y_merge, y_near, y_update, mixing), y_lags)]
     if z_first:
-        more = [(y_first, z_first, *pair) for pair in zip((q_multiply, q_core, q_across, q_merge, q_update, q_mix), q_lags)]
+        more = [(y_first, z_first, *pair) for pair in zip((q_multiply, q_core, q_across, q_merge, q_update, mixing), q_lags)]
         work = [entry for both in zip(work, more) for entry in both]
 
     early = EARLY[distance]
@@ -344,6 +324,13 @@
 
     first = min(lag for _, _, _, lag in work if lag)
     lax.fori_loop(first, max(count + lag for _, count, _, lag in work), body, 0)
+
+    def left(i, carry):
+        size = acc.at[pl.ds(0, 2 * SPAN)]
+        copy(i * SPAN, size, size, core_r.at[0], twin).wait_send()
+        return carry
+
+    lax.fori_loop(0, chunks // SPAN, left, 0)
 
 
 def written(one_ref, two_ref, three_ref, one_out, two_out, three_out, sems):
@@ -379,9 +366,7 @@
     whole = pltpu.VMEM((chunks, 8, rows, LANES), f32)
     shard = pltpu.VMEM((rows, width), f32)
     own = pltpu.VMEM((chunks, rows, LANES), f32)
-    unit = pltpu.VMEM((y_first, 2, rows, LANES), f32)
     single = pltpu.VMEM((y_first, rows, LANES), f32)
-    q_single = pltpu.VMEM((z_slots, rows, LANES), f32)
     out = jax.ShapeDtypeStruct(params.shape, f32)
     anywhere = pl.BlockSpec(memory_space=pl.ANY)
     vmem = pl.BlockSpec(memory_space=pltpu.VMEM)
@@ -400,23 +385,19 @@
             whole,
             whole,
             whole,
-            unit,
-            unit,
-            unit,
+            pltpu.VMEM((y_first, 2, rows, LANES), f32),
+            pltpu.VMEM((y_first, 2, 2, rows, LANES), f32),
             single,
             single,
             pltpu.VMEM((z_slots, RING, rows, LANES), f32),
-            q_single,
-            q_single,
-            q_single,
+            pltpu.VMEM((z_slots, rows, LANES), f32),
+            pltpu.VMEM((z_slots, 2, rows, LANES), f32),
             own,
             own,
             dma((4,)),
+            dma((2 * PREFETCH,)),
+            dma((chunks // SPAN,)),
             dma((chunks,)),
-            dma((chunks,)),
-            dma((chunks,)),
-            dma((chunks, 3)),
-            dma((chunks, 3)),
             dma((chunks,)),
             dma((chunks,)),
             dma((chunks,)),

time: 102 us -> 95.9 us (0.940)
  Pallas kernels: 101 us -> 94.5 us
    pallas_call x1, Pallas kernels: 99 us -> 92.8 us  [fused(): pl.pallas_call(functools.partial(kernel, distance, groups, chunks, rows),...]
where the time goes in v3:
time: 95.9 us; the launch traced here: 95.8 us
  Pallas kernels  94.5 us (99%)
  between operations  1.29 us (1%)
    pallas_call x1, Pallas kernels, fused(): pl.pallas_call(functools.partial(kernel, distance, groups, chunks, rows),...  92.8 us

profile of v3, /device:TPU:1, one launch (start us, length us, event | category | flops | bytes accessed | tf_op | source)
XLA Modules:
  0.0 95.8 jit_solution(2611846670434148596)
XLA Ops:
  1.3 92.9 %conditional.1 = ((f32[1,48,5120]{2,1,0:T(8,128)S(1)}, f32[1,48,5120]{2,1,0:T(8,128)S(1)}, f32[1,48,5120]{2,1,0:T(8,128)S(1)})) conditional(s32[]{:T(128)} %bitcast, (s32[1]{0:T(128)}, s32[1,512]{1,0:T(1,128)}, f32[1,48,5120]{2,1,0:T(8,128)}, f32[1,48,5120]{2,1,0:T(8,128)}, f32[1,48,5120]{2,1,0:T(8,128)}, ...), branch_computations={%region_0.0_spmd, %region_1.0_spmd, %region_2.0_spmd, %region_3.0_... | conditional | flops 4026531840 | bytes 11927560 | solution.py:425
  1.3 92.8 %branch_0_fun.1 = (f32[1,48,5120]{2,1,0:T(8,128)S(1)}, f32[1,48,5120]{2,1,0:T(8,128)S(1)}, f32[1,48,5120]{2,1,0:T(8,128)S(1)}) custom-call(s32[1]{0:T(128)} %get-tuple-element.56.step_ref, s32[1,512]{1,0:T(1,128)} %get-tuple-element.57.ids_ref, f32[1,48,5120]{2,1,0:T(8,128)} %get-tuple-element.58.params_hbm, f32[1,48,5120]{2,1,0:T(8,128)} %get-tuple-element.59.one_hbm, ...), custom_call_target="tpu_custom_call" | custom-call | flops 4026531840 | bytes 11927552 | tf_op jit(solution)/shard_map/cond/branch_0_fun/pallas_call | solution.py:373
  94.2 1.6 %shard_map.94 = (f32[1,48,5120]{2,1,0:T(8,128)}, f32[1,48,5120]{2,1,0:T(8,128)}, f32[1,48,5120]{2,1,0:T(8,128)}) custom-call(f32[1,48,5120]{2,1,0:T(8,128)S(1)} %get-tuple-element.90.one_ref, f32[1,48,5120]{2,1,0:T(8,128)S(1)} %get-tuple-element.91.two_ref, f32[1,48,5120]{2,1,0:T(8,128)S(1)} %get-tuple-element.92.three_ref), custom_call_target="tpu_custom_call" | custom-call | tf_op jit(solution)/shard_map/pallas_call | solution.py:348

commit v4 on v3

--- a/solution.py
+++ b/solution.py
@@ -20,13 +20,14 @@
 PREFETCH = 8
 EARLY = {1: 6, 2: 6, 4: 3, 8: 3}
 STEP_BITS = 16
+REUSE = {1: 16, 2: 16, 4: 12, 8: 12}
 SPAN = 5
 
 PLANS = {
     1: (0, (0, 3, 6, 9, 11, 15), ()),
-    2: (0, (0, 4, 8, 12, 15, 20), ()),
-    4: (18, (0, 2, 5, 8, 11, 15), (0, 2, 6, 9, 12, 16)),
-    8: (18, (0, 2, 5, 8, 11, 15), (0, 2, 6, 9, 12, 16)),
+    2: (0, (0, 3, 6, 9, 11, 17), ()),
+    4: (18, (0, 3, 5, 8, 11, 15), (0, 4, 7, 9, 12, 16)),
+    8: (18, (0, 3, 5, 8, 11, 15), (0, 4, 7, 9, 12, 16)),
 }
 
 
@@ -108,8 +109,14 @@
     hidden_load = pltpu.make_async_copy(hidden_hbm.at[0], hid, load_sem.at[0])
     hidden_load.start()
 
+    def turn(k, count):
+        return jnp.where(k < y_first, k % count, count + (k - y_first) % count)
+
+    def place_of(k):
+        return turn(k, REUSE[distance])
+
     def cot_load(k):
-        slot = jnp.where(k < y_first, k % PREFETCH, PREFETCH + (k - y_first) % PREFETCH)
+        slot = turn(k, PREFETCH)
         columns = pl.ds(pl.multiple_of(k * LANES, LANES), LANES)
         return pltpu.make_async_copy(cot_hbm.at[0, :, columns], cot.at[k], cot_sem.at[slot])
 
@@ -154,7 +161,7 @@
         return pl.ds(pl.multiple_of(k * LANES, LANES), LANES)
 
     def core_copy(k):
-        return copy(k, snd.at[k], r_core.at[k], core_r.at[k], twin)
+        return copy(k, snd.at[k], r_core.at[k], core_r.at[place_of(k)], twin)
 
     def g_copy(k):
         return copy(k, fresh.at[k], g_rcv.at[k], g_r.at[k], below)
@@ -204,16 +211,16 @@
             return acc.at[k, pl.ds(other * 2, 2)]
 
         return (
-            copy(k, of(far), y_far_in.at[k], far_r.at[k], along(to_c)),
-            copy(k, of(to_b), y_near_in.at[k, 0], near_r.at[k], along(to_b)),
-            copy(k, of(to_c), y_near_in.at[k, 1], near_r.at[k], along(to_c)),
+            copy(k, of(far), y_far_in.at[k], far_r.at[place_of(k)], along(to_c)),
+            copy(k, of(to_b), y_near_in.at[k, 0], near_r.at[place_of(k)], along(to_b)),
+            copy(k, of(to_c), y_near_in.at[k, 1], near_r.at[place_of(k)], along(to_c)),
         )
 
     def near_arrived(k, both):
-        copy(k, both, both, near_r.at[k], twin).wait_recv()
+        copy(k, both, both, near_r.at[place_of(k)], twin).wait_recv()
 
     def z_copy(k):
-        return copy(k, z_snd.at[k], z_rcv.at[k], z_r.at[k], across)
+        return copy(k, z_snd.at[k], z_rcv.at[k], z_r.at[place_of(k)], across)
 
     def y_multiply(k, send=True):
         multiply(k, y_first, False, send)
@@ -243,7 +250,7 @@
 
     def q_z_copy(k):
         j = k - y_first
-        return copy(k, acc.at[k, pl.ds((1 - z) * RING, RING)], q_z_in.at[j], z_r.at[k], across)
+        return copy(k, acc.at[k, pl.ds((1 - z) * RING, RING)], q_z_in.at[j], z_r.at[place_of(k)], across)
 
     def q_copies(k):
         j = k - y_first
@@ -253,9 +260,9 @@
             return acc.at[k, z * RING + other]
 
         return (
-            copy(k, of(far), q_far_in.at[j], far_r.at[k], along(to_c)),
-            copy(k, of(to_b), q_near_in.at[j, 0], near_r.at[k], along(to_b)),
-            copy(k, of(to_c), q_near_in.at[j, 1], near_r.at[k], along(to_c)),
+            copy(k, of(far), q_far_in.at[j], far_r.at[place_of(k)], along(to_c)),
+            copy(k, of(to_b), q_near_in.at[j, 0], near_r.at[place_of(k)], along(to_b)),
+            copy(k, of(to_c), q_near_in.at[j, 1], near_r.at[place_of(k)], along(to_c)),
         )
 
     def q_multiply(k, send=True):
@@ -395,12 +402,12 @@
             own,
             own,
             dma((4,)),
-            dma((2 * PREFETCH,)),
+            dma(((2 if z_first else 1) * PREFETCH,)),
             dma((chunks // SPAN,)),
-            dma((chunks,)),
-            dma((chunks,)),
-            dma((chunks,)),
-            dma((chunks,)),
+            dma(((2 if z_first else 1) * REUSE[distance],)),
+            dma(((2 if z_first else 1) * REUSE[distance],)),
+            dma(((2 if z_first else 1) * REUSE[distance],)),
+            dma(((2 if z_first else 1) * REUSE[distance],)),
             dma((chunks,)),
         ],
         compiler_params=pltpu.CompilerParams(

time: 95.9 us -> 95 us (level)
  Pallas kernels: 94.5 us -> 93.5 us
where the time goes in v4:
time: 95 us; the launch traced here: 94.8 us
  Pallas kernels  93.5 us (98%)
  between operations  1.29 us (1%)
    pallas_call x1, Pallas kernels, fused(): pl.pallas_call(functools.partial(kernel, distance, groups, chunks, rows),...  91.9 us

profile of v4, /device:TPU:1, one launch (start us, length us, event | category | flops | bytes accessed | tf_op | source)
XLA Modules:
  0.0 94.8 jit_solution(10904813365284341501)
XLA Ops:
  1.3 91.9 %conditional.1 = ((f32[1,48,5120]{2,1,0:T(8,128)S(1)}, f32[1,48,5120]{2,1,0:T(8,128)S(1)}, f32[1,48,5120]{2,1,0:T(8,128)S(1)})) conditional(s32[]{:T(128)} %bitcast, (s32[1]{0:T(128)}, s32[1,512]{1,0:T(1,128)}, f32[1,48,5120]{2,1,0:T(8,128)}, f32[1,48,5120]{2,1,0:T(8,128)}, f32[1,48,5120]{2,1,0:T(8,128)}, ...), branch_computations={%region_0.0_spmd, %region_1.0_spmd, %region_2.0_spmd, %region_3.0_... | conditional | flops 4026531840 | bytes 11927560 | solution.py:432
  1.3 91.9 %branch_0_fun.1 = (f32[1,48,5120]{2,1,0:T(8,128)S(1)}, f32[1,48,5120]{2,1,0:T(8,128)S(1)}, f32[1,48,5120]{2,1,0:T(8,128)S(1)}) custom-call(s32[1]{0:T(128)} %get-tuple-element.56.step_ref, s32[1,512]{1,0:T(1,128)} %get-tuple-element.57.ids_ref, f32[1,48,5120]{2,1,0:T(8,128)} %get-tuple-element.58.params_hbm, f32[1,48,5120]{2,1,0:T(8,128)} %get-tuple-element.59.one_hbm, ...), custom_call_target="tpu_custom_call" | custom-call | flops 4026531840 | bytes 11927552 | tf_op jit(solution)/shard_map/cond/branch_0_fun/pallas_call | solution.py:380
  93.2 1.6 %shard_map.94 = (f32[1,48,5120]{2,1,0:T(8,128)}, f32[1,48,5120]{2,1,0:T(8,128)}, f32[1,48,5120]{2,1,0:T(8,128)}) custom-call(f32[1,48,5120]{2,1,0:T(8,128)S(1)} %get-tuple-element.90.one_ref, f32[1,48,5120]{2,1,0:T(8,128)S(1)} %get-tuple-element.91.two_ref, f32[1,48,5120]{2,1,0:T(8,128)S(1)} %get-tuple-element.92.three_ref), custom_call_target="tpu_custom_call" | custom-call | tf_op jit(solution)/shard_map/pallas_call | solution.py:355
